TPU v7x, 32 devices: a whole 2x2x4 slice. The times are simulated.
32 devices in a mesh: gx: 4 (over x, core), gy: 8 (over z, y).
Axes of the slice: x: 2, y: 2, z: 4, core: 2. Of those that a mesh axis runs over, the one named last changes fastest.
Arguments:
- fields: float32 [6, 64, 256, 128], P(None, 'gx', 'gy'), may hold values from -6 to 6
- material: int32 [64, 256, 128], P('gx', 'gy'), may hold values from 0 to 15
- ca_table: float32 [16], replicated, may hold values from 0.6 to 1
- cb_table: float32 [16], replicated, may hold values from 0.2 to 0.5
- fine: float32 [4, 8, 8, 2, 128], P('gx', 'gy'), may hold values from -6 to 6
- face_target: int32 [4, 8, 8, 2], P('gx', 'gy'), may hold values from -1 to 511, as said below
- surf_start: int32 [4, 8], P('gx', 'gy'), may hold values from 0 to 24
- surf_count: int32 [4, 8], P('gx', 'gy'), may hold values from 0 to 8, as said below
- omega: float32 [32], replicated, may hold values from 0.3 to 2.5
- bearing: float32 [4096], replicated, may hold values from -3.140625 to 3.140625
Outputs:
- fields_out: float32 [6, 64, 256, 128], P(None, 'gx', 'gy')
- fine_out: float32 [4, 8, 8, 2, 128], P('gx', 'gy')
- far_field: float32 [4, 2, 32, 4096], P('gx')
Inputs may be any that keep to these rules, and one draw needn't show every extreme that they name: `face_target`: live cells of one owner within a gx row are distinct; in each gx row some owner has all 2 slots from every device live. `surf_count`: some device has exactly 8 rows.
All inputs are finite; a program needn't handle non-finite values.
Results may differ from a plain program's by a relative error of at most 0.00017.
Values sent between devices are 32-bit elements; how exact they have to be, the bound alone decides.
A program may use at most 64 MiB of HBM per device.

v0:
```python
import functools
import math

import jax
import jax.numpy as jnp
from jax import lax
from jax.experimental import pallas as pl
from jax.experimental.pallas import tpu as pltpu
from jax.sharding import PartitionSpec as P

STEPS = 4
SY = 8
DTH = 0.5
KAPPA = 0.25
WAVENUM = 0.35
PAD = 8

MESH = pl.DeviceIdType.MESH
HIGH = lax.Precision.HIGHEST


def iota(shape, dim):
    return lax.broadcasted_iota(jnp.int32, shape, dim)


def rows_up(value, last):
    count = value.shape[0]
    return jnp.where(iota(value.shape, 0) == count - 1, last, pltpu.roll(value, count - 1, 0))


def z_up(value):
    count = value.shape[1]
    return jnp.where(iota(value.shape, 1) == count - 1, 0.0, pltpu.roll(value, count - 1, 1))


def z_down(value):
    return jnp.where(iota(value.shape, 1) == 0, 0.0, pltpu.roll(value, 1, 1))


def kernel(
    n_x, n_y,
    fields, material, fine, bearing, ca_table, cb_table, target, start, count, omega,
    fields_out, fine_out, far_out,
    e_buf, h_buf, ca_buf, cb_buf, fd_buf, mk_buf, mat,
    xt, xh, yt, yh, c1, c2, gx_in, gy_in,
    syt, syh, sgy, sc1, sc2,
    s_all, fin, fpad, fback, fhome, table, yc, ys, w_buf, g_all, far_buf,
    load_sem, send_sem, recv_sem, s_send, s_recv, f_send, f_recv, g_send, g_recv, out_sem,
):
    _, cx, cy, nz = fields.shape
    slots = fine.shape[1]
    local_a = g_all.shape[2]
    freqs = omega.shape[0]
    gx = lax.axis_index("gx")
    gy = lax.axis_index("gy")
    has_l, has_r = gx > 0, gx < n_x - 1
    has_d, has_u = gy > 0, gy < n_y - 1
    left, right = (gx - 1, gy), (gx + 1, gy)
    down, up = (gx, gy - 1), (gx, gy + 1)
    left_up, right_down = (gx - 1, gy + 1), (gx + 1, gy - 1)
    has_lu, has_rd = has_l & has_u, has_r & has_d

    loads = [
        pltpu.make_async_copy(fields.at[0:3], e_buf.at[:, 0:cx, 0:cy], load_sem.at[0]),
        pltpu.make_async_copy(fields.at[3:6], h_buf.at[:, 1 : cx + 1, PAD : PAD + cy], load_sem.at[1]),
        pltpu.make_async_copy(material, mat, load_sem.at[2]),
        pltpu.make_async_copy(fine.at[gy], fin.at[gy], load_sem.at[3]),
    ]
    for load in loads:
        load.start()

    barrier = pltpu.get_barrier_semaphore()
    for has, where in ((has_l, left), (has_r, right), (has_lu, left_up), (has_rd, right_down)):

        @pl.when(has)
        def _(where=where):
            pl.semaphore_signal(barrier, inc=1, device_id=where, device_id_type=MESH)

    def peer_of(k):
        return lax.rem(gy + k, n_y)

    def greet(k, carry):
        pl.semaphore_signal(barrier, inc=1, device_id=(gx, peer_of(k)), device_id_type=MESH)
        return carry

    lax.fori_loop(1, n_y, greet, 0)

    for has, refs in (
        (has_l, (xt, gx_in)), (has_r, (xh,)), (has_d, (yt, gy_in)), (has_u, (yh,)), (has_lu, (c1,)), (has_rd, (c2,)),
    ):

        @pl.when(jnp.logical_not(has))
        def _(refs=refs):
            for ref in refs:
                ref[...] = jnp.zeros(ref.shape, ref.dtype)

    s_all[STEPS, gy] = jnp.broadcast_to(start[0, 0].astype(jnp.float32), (SY, nz))
    arrivals = (
        has_l.astype(jnp.int32) + has_r.astype(jnp.int32) + has_lu.astype(jnp.int32) + has_rd.astype(jnp.int32)
    )
    pl.semaphore_wait(barrier, arrivals + (n_y - 1))

    def remote(index, src, dst, where):
        return pltpu.make_async_remote_copy(
            src_ref=src, dst_ref=dst, send_sem=send_sem.at[index], recv_sem=recv_sem.at[index],
            device_id=where, device_id_type=MESH,
        )

    def x_copies(t, src_tail, src_head):
        return [
            (has_r, has_l, remote(6 * t + 0, src_tail, xt.at[t], right)),
            (has_l, has_r, remote(6 * t + 1, src_head, xh.at[t], left)),
        ]

    def y_copies(t):
        return [
            (has_u, has_d, remote(6 * t + 2, syt.at[t], yt.at[t], up)),
            (has_d, has_u, remote(6 * t + 3, syh.at[t], yh.at[t], down)),
            (has_rd, has_lu, remote(6 * t + 4, sc1.at[t], c1.at[t], right_down)),
            (has_lu, has_rd, remote(6 * t + 5, sc2.at[t], c2.at[t], left_up)),
        ]

    def begin(copies):
        for sends, _, copy in copies:

            @pl.when(sends)
            def _(copy=copy):
                copy.start()

    def arrived(copies):
        for _, comes, copy in copies:

            @pl.when(comes)
            def _(copy=copy):
                copy.wait_recv()

    def sent(copies):
        for sends, _, copy in copies:

            @pl.when(sends)
            def _(copy=copy):
                copy.wait_send()

    def to_peers(src_of, dst, sends, recvs):
        def one(k, carry):
            peer = peer_of(k)
            pltpu.make_async_remote_copy(
                src_ref=src_of(peer), dst_ref=dst, send_sem=sends, recv_sem=recvs,
                device_id=(gx, peer), device_id_type=MESH,
            ).start()
            return carry

        lax.fori_loop(1, n_y, one, 0)

    def wait_all(ref, sem):
        part = ref.at[0 : n_y - 1]
        pltpu.make_async_copy(part, part, sem).wait()

    x_now = x_copies(0, fields.at[0:3, cx - 1], fields.at[1:3, 0])
    x_now.append((has_r, has_l, remote(6 * STEPS, fields.at[4:6, cx - 1], gx_in, right)))
    begin(x_now)
    to_peers(lambda peer: fine.at[peer], fin.at[gy], f_send.at[0], f_recv.at[0])
    to_peers(lambda peer: s_all.at[STEPS, gy], s_all.at[STEPS, gy], s_send.at[STEPS], s_recv.at[STEPS])

    for load in loads[:2]:
        load.wait()

    def stage(x, carry):
        for comp in range(3):
            syt[0, comp, pl.ds(x, 1), :] = e_buf[comp, x, cy - 1 : cy, :]
        syh[0, 0, pl.ds(x, 1), :] = e_buf[0, x, 0:1, :]
        syh[0, 1, pl.ds(x, 1), :] = e_buf[2, x, 0:1, :]
        sgy[0, pl.ds(x, 1), :] = h_buf[0, x + 1, PAD + cy - 1 : PAD + cy, :]
        sgy[1, pl.ds(x, 1), :] = h_buf[2, x + 1, PAD + cy - 1 : PAD + cy, :]
        return carry

    lax.fori_loop(0, cx, stage, 0)

    def stage_corners(t):
        sc1[t] = jnp.broadcast_to(e_buf[0, cx - 1, 0:1, :], (8, nz))
        sc2[t] = jnp.broadcast_to(e_buf[1, 0, cy - 1 : cy, :], (8, nz))

    stage_corners(0)
    y_now = y_copies(0)
    y_now.append((has_u, has_d, remote(6 * STEPS + 1, sgy, gy_in, up)))
    begin(y_now)

    for load in loads[2:]:
        load.wait()

    def look_up(x, carry):
        index = mat[x]
        ca = jnp.zeros((cy, nz), jnp.float32)
        cb = jnp.zeros((cy, nz), jnp.float32)
        for m in range(ca_table.shape[0]):
            chosen = index == m
            ca = jnp.where(chosen, ca_table[m], ca)
            cb = jnp.where(chosen, cb_table[m], cb)
        ca_buf[x] = ca
        cb_buf[x] = cb
        return carry

    lax.fori_loop(0, cx, look_up, 0)

    angle = bearing[:, pl.ds(pl.multiple_of(gy * local_a, local_a), local_a)]
    cos_b, sin_b = jnp.cos(angle), jnp.sin(angle)
    arg_low = (WAVENUM * iota((8, local_a), 0).astype(jnp.float32)) * cos_b
    cos_low, sin_low = jnp.cos(arg_low), jnp.sin(arg_low)
    tops = nz // 8
    arg_top = ((WAVENUM * 8) * iota((tops, local_a), 0).astype(jnp.float32)) * cos_b
    cos_top, sin_top = jnp.cos(arg_top), jnp.sin(arg_top)
    for top in range(tops):
        ct, st = cos_top[top : top + 1], sin_top[top : top + 1]
        table[8 * top : 8 * top + 8, 0:local_a] = ct * cos_low - st * sin_low
        table[8 * top : 8 * top + 8, local_a : 2 * local_a] = st * cos_low + ct * sin_low

    wait_all(fin, f_recv.at[0])
    fpad[...] = jnp.zeros(fpad.shape, jnp.float32)
    wide = fpad.shape[0]
    lane = iota((1, wide), 1)
    cell_row = jnp.full((1, wide), -1, jnp.int32)
    for holder in range(n_y):
        fpad[slots * holder : slots * (holder + 1), :] = fin[holder]
        for slot in range(slots):
            cell_row = jnp.where(lane == slots * holder + slot, target[holder, slot], cell_row)
    onehot = (iota((cx * cy, wide), 0) == cell_row).astype(jnp.float32).astype(jnp.bfloat16)
    rest = fpad[...]
    dense = jnp.zeros((cx * cy, nz), jnp.float32)
    for _ in range(3):
        part = rest.astype(jnp.bfloat16)
        rest = rest - part.astype(jnp.float32)
        dense = dense + jnp.dot(onehot, part, preferred_element_type=jnp.float32)
    fd_buf[...] = dense
    mk_buf[...] = jnp.dot(
        onehot, jnp.full((wide, nz), KAPPA, jnp.bfloat16), preferred_element_type=jnp.float32
    )

    om = jnp.zeros((freqs, 128), jnp.float32)
    for f in range(freqs):
        om = jnp.where(iota((freqs, 128), 0) == f, omega[f], om)
    lanes = iota((freqs, 128), 1)
    second = lanes >= STEPS
    tick_of = jnp.where(second, lanes - STEPS, lanes) + 1
    moment = om * tick_of.astype(jnp.float32)
    norm = 1.0 / math.sqrt(n_y * SY * nz)
    cos_m, sin_m = jnp.cos(moment) * norm, jnp.sin(moment) * norm
    w_buf[0:freqs, :] = jnp.where(second, sin_m, cos_m)
    w_buf[freqs : 2 * freqs, :] = jnp.where(second, cos_m, -sin_m)

    wait_all(s_all.at[STEPS], s_recv.at[STEPS])
    row_count = n_y * SY
    row = iota((row_count, nz), 0)
    spot = s_all[STEPS].reshape(row_count, nz) + ((row // SY) * cy + lax.rem(row, SY)).astype(jnp.float32)
    arg_y = (WAVENUM * spot[:, 0:1]) * sin_b
    yc[...] = jnp.cos(arg_y)
    ys[...] = jnp.sin(arg_y)

    keep_l = has_l.astype(jnp.float32)
    keep_d = has_d.astype(jnp.float32)
    row_mask = (iota((SY, nz), 0) < count[0, 0]).astype(jnp.float32)

    for t in range(STEPS):
        arrived(x_now)
        arrived(y_now)
        sent(x_now)
        if t == 0:
            h_buf[1, 0, PAD : PAD + cy, :] = gx_in[0]
            h_buf[2, 0, PAD : PAD + cy, :] = gx_in[1]
        ex, ey, ez = xt[t, 0], xt[t, 1], xt[t, 2]
        hy = h_buf[1, 0, PAD : PAD + cy, :]
        hz = h_buf[2, 0, PAD : PAD + cy, :]
        ahead = rows_up(ex, c1[t, 0:1, :])
        h_buf[1, 0, PAD : PAD + cy, :] = keep_l * (
            hy - DTH * ((z_up(ex) - ex) - (e_buf[2, 0, 0:cy, :] - ez))
        )
        h_buf[2, 0, PAD : PAD + cy, :] = keep_l * (
            hz - DTH * ((e_buf[1, 0, 0:cy, :] - ey) - (ahead - ex))
        )
        ex, ey, ez = yt[t, 0], yt[t, 1], yt[t, 2]
        ahead = rows_up(ey, c2[t, 0:1, :])
        gy_in[0] = keep_d * (gy_in[0] - DTH * ((syh[t, 1] - ez) - (z_up(ey) - ey)))
        gy_in[1] = keep_d * (gy_in[1] - DTH * ((ahead - ey) - (syh[t, 0] - ex)))
        e_buf[1, cx, 0:cy, :] = xh[t, 0]
        e_buf[2, cx, 0:cy, :] = xh[t, 1]

        def edges(x, carry, t=t):
            e_buf[0, x, cy : cy + 1, :] = yh[t, 0, pl.ds(x, 1), :]
            e_buf[2, x, cy : cy + 1, :] = yh[t, 1, pl.ds(x, 1), :]
            h_buf[0, x + 1, PAD - 1 : PAD, :] = gy_in[0, pl.ds(x, 1), :]
            h_buf[2, x + 1, PAD - 1 : PAD, :] = gy_in[1, pl.ds(x, 1), :]
            return carry

        lax.fori_loop(0, cx, edges, 0)

        def h_plane(x, carry):
            own = slice(PAD, PAD + cy)
            ex, ey, ez = (e_buf[comp, x, 0:cy, :] for comp in range(3))
            ex_y, ez_y = e_buf[0, x, 1 : cy + 1, :], e_buf[2, x, 1 : cy + 1, :]
            ey_x, ez_x = e_buf[1, x + 1, 0:cy, :], e_buf[2, x + 1, 0:cy, :]
            h_buf[0, x + 1, own, :] = h_buf[0, x + 1, own, :] - DTH * ((ez_y - ez) - (z_up(ey) - ey))
            h_buf[1, x + 1, own, :] = h_buf[1, x + 1, own, :] - DTH * ((z_up(ex) - ex) - (ez_x - ez))
            h_buf[2, x + 1, own, :] = h_buf[2, x + 1, own, :] - DTH * ((ey_x - ey) - (ex_y - ex))
            return carry

        lax.fori_loop(0, cx, h_plane, 0)

        def e_plane(x, carry, t=t):
            own = slice(PAD, PAD + cy)
            before = slice(PAD - 1, PAD + cy - 1)
            hx, hy, hz = (h_buf[comp, x + 1, own, :] for comp in range(3))
            hx_y, hz_y = h_buf[0, x + 1, before, :], h_buf[2, x + 1, before, :]
            hy_x, hz_x = h_buf[1, x, own, :], h_buf[2, x, own, :]
            ca, cb = ca_buf[x], cb_buf[x]
            ex = ca * e_buf[0, x, 0:cy, :] + cb * ((hz - hz_y) - (hy - z_down(hy)))
            ey = ca * e_buf[1, x, 0:cy, :] + cb * ((hx - z_down(hx)) - (hz - hz_x))
            ez = ca * e_buf[2, x, 0:cy, :] + cb * ((hy - hy_x) - (hx - hx_y))
            cells = pl.ds(pl.multiple_of(x * cy, cy), cy)
            mk, fd = mk_buf[cells, :], fd_buf[cells, :]
            ez = ez + mk * (fd - ez)
            fd_buf[cells, :] = fd + (2.0 * mk) * (ez - fd)
            e_buf[0, x, 0:cy, :] = ex
            e_buf[1, x, 0:cy, :] = ey
            e_buf[2, x, 0:cy, :] = ez
            if t + 1 < STEPS:
                syt[t + 1, 0, pl.ds(x, 1), :] = ex[cy - 1 : cy]
                syt[t + 1, 1, pl.ds(x, 1), :] = ey[cy - 1 : cy]
                syt[t + 1, 2, pl.ds(x, 1), :] = ez[cy - 1 : cy]
                syh[t + 1, 0, pl.ds(x, 1), :] = ex[0:1]
                syh[t + 1, 1, pl.ds(x, 1), :] = ez[0:1]
            return carry

        lax.fori_loop(0, cx, e_plane, 0)
        sent(y_now)
        if t + 1 < STEPS:
            stage_corners(t + 1)
            y_now = y_copies(t + 1)
            begin(y_now)
            x_now = x_copies(t + 1, e_buf.at[:, cx - 1, 0:cy], e_buf.at[1:3, 0, 0:cy])
            begin(x_now)
        first = start[0, 0]
        s_all[t, gy] = row_mask * (
            e_buf[2, 0, pl.ds(first, SY), :] + h_buf[1, 1, pl.ds(PAD + first, SY), :]
        )
        to_peers(lambda peer, t=t: s_all.at[t, gy], s_all.at[t, gy], s_send.at[t], s_recv.at[t])

    stores = [
        pltpu.make_async_copy(e_buf.at[:, 0:cx, 0:cy], fields_out.at[0:3], out_sem.at[0]),
        pltpu.make_async_copy(h_buf.at[:, 1 : cx + 1, PAD : PAD + cy], fields_out.at[3:6], out_sem.at[1]),
    ]
    for store in stores:
        store.start()

    for holder in range(n_y):
        for slot in range(slots):
            cell = target[holder, slot]
            line = fd_buf[pl.ds(jnp.maximum(cell, 0), 1), :]
            alive = jnp.broadcast_to(cell, (1, nz)) >= 0
            fback[holder, slot : slot + 1, :] = jnp.where(alive, line, fin[holder, slot : slot + 1, :])
    to_peers(lambda peer: fback.at[peer], fhome.at[gy], f_send.at[1], f_recv.at[1])
    fhome[gy] = fback[gy]

    for t in range(STEPS):
        wait_all(s_all.at[t], s_recv.at[t])
        q = jnp.dot(s_all[t].reshape(row_count, nz), table[...], precision=HIGH, preferred_element_type=jnp.float32)
        q_real, q_imag = q[:, 0:local_a], q[:, local_a : 2 * local_a]
        g_all[gy, t : t + 1, :] = jnp.sum(q_real * yc[...] - q_imag * ys[...], axis=0, keepdims=True)
        g_all[gy, STEPS + t : STEPS + t + 1, :] = jnp.sum(q_real * ys[...] + q_imag * yc[...], axis=0, keepdims=True)
    to_peers(lambda peer: g_all.at[gy], g_all.at[gy], g_send, g_recv)
    wait_all(fhome, f_recv.at[1])
    home = pltpu.make_async_copy(fhome, fine_out, out_sem.at[2])
    home.start()
    wait_all(g_all, g_recv)
    weights = w_buf[:, 0 : 2 * STEPS]
    for part in range(n_y):
        far_buf[:, part * local_a : (part + 1) * local_a] = jnp.dot(
            weights, g_all[part], precision=HIGH, preferred_element_type=jnp.float32
        )
    far = pltpu.make_async_copy(far_buf, far_out, out_sem.at[3])
    far.start()

    wait_all(fin, f_send.at[0])
    wait_all(fhome, f_send.at[1])
    for t in range(STEPS + 1):
        wait_all(s_all.at[t], s_send.at[t])
    wait_all(g_all, g_send)
    for store in stores:
        store.wait()
    home.wait()
    far.wait()


def shards(
    n_x, n_y, fields, material, ca_table, cb_table, fine, face_target, surf_start, surf_count, omega, bearing
):
    _, cx, cy, nz = fields.shape
    slots = fine.shape[3]
    freqs, angles = omega.shape[0], bearing.shape[0]
    local_a = angles // n_y
    wide = -(-n_y * slots // 128) * 128
    f32 = jnp.float32
    vmem = lambda *shape: pltpu.VMEM(shape, f32)
    dma = pltpu.SemaphoreType.DMA
    any_space = pl.BlockSpec(memory_space=pl.ANY)
    smem = pl.BlockSpec(memory_space=pltpu.SMEM)
    scratch = [
        vmem(3, cx + 1, cy + PAD, nz),
        vmem(3, cx + 1, cy + PAD, nz),
        vmem(cx, cy, nz),
        vmem(cx, cy, nz),
        vmem(cx * cy, nz),
        vmem(cx * cy, nz),
        pltpu.VMEM((cx, cy, nz), jnp.int32),
        vmem(STEPS, 3, cy, nz),
        vmem(STEPS, 2, cy, nz),
        vmem(STEPS, 3, cx, nz),
        vmem(STEPS, 2, cx, nz),
        vmem(STEPS, 8, nz),
        vmem(STEPS, 8, nz),
        vmem(2, cy, nz),
        vmem(2, cx, nz),
        vmem(STEPS, 3, cx, nz),
        vmem(STEPS, 2, cx, nz),
        vmem(2, cx, nz),
        vmem(STEPS, 8, nz),
        vmem(STEPS, 8, nz),
        vmem(STEPS + 1, n_y, SY, nz),
        vmem(n_y, slots, nz),
        vmem(wide, nz),
        vmem(n_y, slots, nz),
        vmem(n_y, slots, nz),
        vmem(nz, 2 * local_a),
        vmem(n_y * SY, local_a),
        vmem(n_y * SY, local_a),
        vmem(2 * freqs, 128),
        vmem(n_y, 2 * STEPS, local_a),
        vmem(2 * freqs, angles),
        dma((4,)),
        dma((6 * STEPS + 2,)),
        dma((6 * STEPS + 2,)),
        dma((STEPS + 1,)),
        dma((STEPS + 1,)),
        dma((2,)),
        dma((2,)),
        dma(()),
        dma(()),
        dma((4,)),
    ]
    out, fine_new, far = pl.pallas_call(
        functools.partial(kernel, n_x, n_y),
        out_shape=(
            jax.ShapeDtypeStruct(fields.shape, f32),
            jax.ShapeDtypeStruct((n_y, slots, nz), f32),
            jax.ShapeDtypeStruct((2 * freqs, angles), f32),
        ),
        in_specs=[any_space] * 3 + [pl.BlockSpec(memory_space=pltpu.VMEM)] + [smem] * 6,
        out_specs=(any_space,) * 3,
        scratch_shapes=scratch,
        compiler_params=pltpu.CompilerParams(
            collective_id=0, has_side_effects=True, vmem_limit_bytes=40 * 1024 * 1024
        ),
    )(
        fields, material, fine.reshape(n_y, slots, nz), bearing.reshape(1, angles),
        ca_table, cb_table, face_target.reshape(n_y, slots), surf_start, surf_count, omega,
    )
    return out, fine_new.reshape(fine.shape), far.reshape(1, 2, freqs, angles)


def solution(mesh):
    in_specs = (
        P(None, "gx", "gy", None),
        P("gx", "gy", None),
        P(),
        P(),
        P("gx", "gy", None, None, None),
        P("gx", "gy", None, None),
        P("gx", "gy"),
        P("gx", "gy"),
        P(),
        P(),
    )
    out_specs = (
        P(None, "gx", "gy", None),
        P("gx", "gy", None, None, None),
        P("gx", None, None, None),
    )
    body = functools.partial(shards, mesh.shape["gx"], mesh.shape["gy"])
    return jax.shard_map(body, mesh=mesh, in_specs=in_specs, out_specs=out_specs, check_vma=False)
```

profile of v0, /device:TPU:0, one launch (start us, length us, event | category | flops | bytes accessed | tf_op | source)
XLA Modules:
  0.0 54.2 jit_solution(8553535397974165632)
XLA Ops:
  1.9 0.8 %copy.13.target = s32[8,2]{1,0:T(8,128)S(1)} copy(s32[8,2]{0,1:T(2,128)} %bitcast.9) | data formatting | bytes 128 | tf_op jit(solution)/shard_map/reshape | solution.py:463
  2.7 0.0 copy-start
  2.7 1.4 %copy-done = f32[6,16,32,128]{3,2,1,0:T(8,128)S(1)} copy-done((f32[6,16,32,128]{3,2,1,0:T(8,128)S(1)}, f32[6,16,32,128]{3,2,1,0:T(8,128)}, u32[]{:S(2)}) %copy-start) | copy-done | bytes 1572888
  4.1 0.0 copy-start.1
  4.1 0.9 %copy-done.1 = s32[16,32,128]{2,1,0:T(8,128)S(1)} copy-done((s32[16,32,128]{2,1,0:T(8,128)S(1)}, s32[16,32,128]{2,1,0:T(8,128)}, u32[]{:S(2)}) %copy-start.1) | copy-done | bytes 262168
  5.0 0.0 copy-start.2
  5.0 0.7 %copy-done.2 = f32[4096]{0:T(1024)S(1)} copy-done((f32[4096]{0:T(1024)S(1)}, f32[4096]{0:T(1024)}, u32[]{:S(2)}) %copy-start.2) | copy-done | bytes 16408
  5.8 0.0 copy-start.3
  5.8 0.7 %copy-done.3 = f32[1,1,8,2,128]{4,3,2,1,0:T(2,128)S(1)} copy-done((f32[1,1,8,2,128]{4,3,2,1,0:T(2,128)S(1)}, f32[1,1,8,2,128]{4,3,2,1,0:T(2,128)}, u32[]{:S(2)}) %copy-start.3) | copy-done | bytes 8216
  6.5 0.0 copy-start.4
  6.5 0.7 %copy-done.4 = f32[16]{0:T(128)S(1)} copy-done((f32[16]{0:T(128)S(1)}, f32[16]{0:T(128)}, u32[]{:S(2)}) %copy-start.4) | copy-done | bytes 88
  7.1 0.0 copy-start.5
  7.1 0.7 %copy-done.5 = f32[16]{0:T(128)S(1)} copy-done((f32[16]{0:T(128)S(1)}, f32[16]{0:T(128)}, u32[]{:S(2)}) %copy-start.5) | copy-done | bytes 88
  7.8 0.0 copy-start.6
  7.8 0.7 %copy-done.6 = f32[32]{0:T(128)S(1)} copy-done((f32[32]{0:T(128)S(1)}, f32[32]{0:T(128)}, u32[]{:S(2)}) %copy-start.6) | copy-done | bytes 152
  8.4 43.0 %shard_map.121 = (f32[6,16,32,128]{3,2,1,0:T(8,128)S(1)}, f32[8,2,128]{2,1,0:T(2,128)S(1)}, f32[64,4096]{1,0:T(8,128)S(1)}) custom-call(f32[6,16,32,128]{3,2,1,0:T(8,128)S(1)} %copy-done, s32[16,32,128]{2,1,0:T(8,128)S(1)} %copy-done.1, f32[8,2,128]{2,1,0:T(2,128)S(1)} %bitcast.7, f32[1,4096]{1,0:T(1,128)S(1)} %bitcast.6, f32[16]{0:T(128)S(1)} %copy-done.4, ...), custom_call_target="tpu_custom_call" | custom-call | tf_op jit(solution)/shard_map/pallas_call | solution.py:448
  51.4 1.1 %copy.19 = f32[6,16,32,128]{3,2,1,0:T(8,128)} copy(f32[6,16,32,128]{3,2,1,0:T(8,128)S(1)} %get-tuple-element.12) | data formatting | bytes 3145728
  52.6 0.6 %copy.20 = f32[1,1,8,2,128]{4,3,2,1,0:T(2,128)} copy(f32[1,1,8,2,128]{4,3,2,1,0:T(2,128)S(1)} %bitcast.8) | data formatting | bytes 16384
  53.2 1.0 %copy.21 = f32[1,2,32,4096]{3,2,1,0:T(8,128)} copy(f32[1,2,32,4096]{3,2,1,0:T(8,128)S(1)} %bitcast.5) | data formatting | bytes 2097152
Async XLA Ops:
  2.7 1.4 %copy-start = (f32[6,16,32,128]{3,2,1,0:T(8,128)S(1)}, f32[6,16,32,128]{3,2,1,0:T(8,128)}, u32[]{:S(2)}) copy-start(f32[6,16,32,128]{3,2,1,0:T(8,128)} %fields.1) | copy-start | bytes 4718596
  4.1 0.9 %copy-start.1 = (s32[16,32,128]{2,1,0:T(8,128)S(1)}, s32[16,32,128]{2,1,0:T(8,128)}, u32[]{:S(2)}) copy-start(s32[16,32,128]{2,1,0:T(8,128)} %material.1) | copy-start | bytes 786436
  5.0 0.7 %copy-start.2 = (f32[4096]{0:T(1024)S(1)}, f32[4096]{0:T(1024)}, u32[]{:S(2)}) copy-start(f32[4096]{0:T(1024)} %param.19) | copy-start | bytes 49156
  5.8 0.7 %copy-start.3 = (f32[1,1,8,2,128]{4,3,2,1,0:T(2,128)S(1)}, f32[1,1,8,2,128]{4,3,2,1,0:T(2,128)}, u32[]{:S(2)}) copy-start(f32[1,1,8,2,128]{4,3,2,1,0:T(2,128)} %param.14) | copy-start | bytes 24580
  6.5 0.7 %copy-start.4 = (f32[16]{0:T(128)S(1)}, f32[16]{0:T(128)}, u32[]{:S(2)}) copy-start(f32[16]{0:T(128)} %ca_table.1) | copy-start | bytes 196
  7.1 0.7 %copy-start.5 = (f32[16]{0:T(128)S(1)}, f32[16]{0:T(128)}, u32[]{:S(2)}) copy-start(f32[16]{0:T(128)} %cb_table.1) | copy-start | bytes 196
  7.8 0.7 %copy-start.6 = (f32[32]{0:T(128)S(1)}, f32[32]{0:T(128)}, u32[]{:S(2)}) copy-start(f32[32]{0:T(128)} %omega.1) | copy-start | bytes 388
where the time goes:
time: 54.5 us; the launch traced here: 54.2 us
  Pallas kernels  43 us (79%)
  local copies, waits for them, and re-layouts  9.2 us (17%)
  between operations  1.94 us (4%)
    pallas_call x1, Pallas kernels, shards(): pl.pallas_call(functools.partial(kernel, n_x, n_y), out_shape=(jax.ShapeD...  43 us
    unnamed x17, local copies, waits for them, and re-layouts  8.45 us

commit v1 on v0

--- a/solution.py
+++ b/solution.py
@@ -39,13 +39,14 @@
 
 def kernel(
     n_x, n_y,
-    fields, material, fine, bearing, ca_table, cb_table, target, start, count, omega,
+    fields, material, fine, bearing_in, ca_in, cb_in, target_in, start_in, count_in, omega_in,
     fields_out, fine_out, far_out,
     e_buf, h_buf, ca_buf, cb_buf, fd_buf, mk_buf, mat,
     xt, xh, yt, yh, c1, c2, gx_in, gy_in,
     syt, syh, sgy, sc1, sc2,
-    s_all, fin, fpad, fback, fhome, table, yc, ys, w_buf, g_all, far_buf,
-    load_sem, send_sem, recv_sem, s_send, s_recv, f_send, f_recv, g_send, g_recv, out_sem,
+    s_all, fin, fpad, fback, fhome, table, yc, ys, w_buf, g_all, hrow,
+    bearing, ca_table, cb_table, target, start, count, omega,
+    load_sem, send_sem, recv_sem, s_send, s_recv, f_send, f_recv, g_send, g_recv, small_sem,
 ):
     _, cx, cy, nz = fields.shape
     slots = fine.shape[1]
@@ -66,8 +67,16 @@
         pltpu.make_async_copy(material, mat, load_sem.at[2]),
         pltpu.make_async_copy(fine.at[gy], fin.at[gy], load_sem.at[3]),
     ]
-    for load in loads:
+    small = [
+        pltpu.make_async_copy(src, dst, small_sem.at[index])
+        for index, (src, dst) in enumerate((
+            (bearing_in, bearing), (ca_in, ca_table), (cb_in, cb_table), (target_in, target),
+            (start_in, start), (count_in, count), (omega_in, omega),
+        ))
+    ]
+    for load in loads + small:
         load.start()
+    e_buf[:, 0:cx, cy : cy + PAD, :] = jnp.zeros((3, cx, PAD, nz), jnp.float32)
 
     barrier = pltpu.get_barrier_semaphore()
     for has, where in ((has_l, left), (has_r, right), (has_lu, left_up), (has_rd, right_down)):
@@ -94,6 +103,8 @@
             for ref in refs:
                 ref[...] = jnp.zeros(ref.shape, ref.dtype)
 
+    for load in small:
+        load.wait()
     s_all[STEPS, gy] = jnp.broadcast_to(start[0, 0].astype(jnp.float32), (SY, nz))
     arrivals = (
         has_l.astype(jnp.int32) + has_r.astype(jnp.int32) + has_lu.astype(jnp.int32) + has_rd.astype(jnp.int32)
@@ -165,16 +176,18 @@
     for load in loads[:2]:
         load.wait()
 
-    def stage(x, carry):
+    def stage(x):
         for comp in range(3):
             syt[0, comp, pl.ds(x, 1), :] = e_buf[comp, x, cy - 1 : cy, :]
         syh[0, 0, pl.ds(x, 1), :] = e_buf[0, x, 0:1, :]
         syh[0, 1, pl.ds(x, 1), :] = e_buf[2, x, 0:1, :]
-        sgy[0, pl.ds(x, 1), :] = h_buf[0, x + 1, PAD + cy - 1 : PAD + cy, :]
-        sgy[1, pl.ds(x, 1), :] = h_buf[2, x + 1, PAD + cy - 1 : PAD + cy, :]
-        return carry
-
-    lax.fori_loop(0, cx, stage, 0)
+        for part, comp in enumerate((0, 2)):
+            line = h_buf[comp, x + 1, PAD + cy - 1 : PAD + cy, :]
+            sgy[part, pl.ds(x, 1), :] = line
+            hrow[part, pl.ds(x, 1), :] = line
+
+    for x in range(cx):
+        stage(x)
 
     def stage_corners(t):
         sc1[t] = jnp.broadcast_to(e_buf[0, cx - 1, 0:1, :], (8, nz))
@@ -184,6 +197,29 @@
     y_now = y_copies(0)
     y_now.append((has_u, has_d, remote(6 * STEPS + 1, sgy, gy_in, up)))
     begin(y_now)
+    own = slice(PAD, PAD + cy)
+
+    def h_plane(x, ey_x, ez_x):
+        ex, ey, ez = (e_buf[comp, x, 0:cy, :] for comp in range(3))
+        ex_y, ez_y = e_buf[0, x, 1 : cy + 1, :], e_buf[2, x, 1 : cy + 1, :]
+        h_buf[0, x + 1, own, :] = h_buf[0, x + 1, own, :] - DTH * ((ez_y - ez) - (z_up(ey) - ey))
+        h_buf[1, x + 1, own, :] = h_buf[1, x + 1, own, :] - DTH * ((z_up(ex) - ex) - (ez_x - ez))
+        h_buf[2, x + 1, own, :] = h_buf[2, x + 1, own, :] - DTH * ((ey_x - ey) - (ex_y - ex))
+
+    def planes(first, last, one, most=5):
+        group = max(k for k in range(1, most + 1) if (last - first) % k == 0)
+
+        def several(index, carry):
+            for k in range(group):
+                one(first + index * group + k)
+            return carry
+
+        lax.fori_loop(0, (last - first) // group, several, 0)
+
+    def h_inside():
+        planes(0, cx - 1, lambda x: h_plane(x, e_buf[1, x + 1, 0:cy, :], e_buf[2, x + 1, 0:cy, :]))
+
+    h_inside()
 
     for load in loads[2:]:
         load.wait()
@@ -222,7 +258,7 @@
     for holder in range(n_y):
         fpad[slots * holder : slots * (holder + 1), :] = fin[holder]
         for slot in range(slots):
-            cell_row = jnp.where(lane == slots * holder + slot, target[holder, slot], cell_row)
+            cell_row = jnp.where(lane == slots * holder + slot, target[slot, holder], cell_row)
     onehot = (iota((cx * cy, wide), 0) == cell_row).astype(jnp.float32).astype(jnp.bfloat16)
     rest = fpad[...]
     dense = jnp.zeros((cx * cy, nz), jnp.float32)
@@ -259,53 +295,58 @@
     keep_d = has_d.astype(jnp.float32)
     row_mask = (iota((SY, nz), 0) < count[0, 0]).astype(jnp.float32)
 
+    def far_tick(t):
+        wait_all(s_all.at[t], s_recv.at[t])
+        q = jnp.dot(s_all[t].reshape(row_count, nz), table[...], precision=HIGH, preferred_element_type=jnp.float32)
+        q_real, q_imag = q[:, 0:local_a], q[:, local_a : 2 * local_a]
+        g_all[gy, t : t + 1, :] = jnp.sum(q_real * yc[...] - q_imag * ys[...], axis=0, keepdims=True)
+        g_all[gy, STEPS + t : STEPS + t + 1, :] = jnp.sum(q_real * ys[...] + q_imag * yc[...], axis=0, keepdims=True)
+
+    def send_surface(t):
+        to_peers(lambda peer: s_all.at[t, gy], s_all.at[t, gy], s_send.at[t], s_recv.at[t])
+
+    def keep_surface(t, e_ref):
+        first = start[0, 0]
+        s_all[t, gy] = row_mask * (
+            e_ref[2, 0, pl.ds(first, SY), :] + h_buf[1, 1, pl.ds(PAD + first, SY), :]
+        )
+
     for t in range(STEPS):
+        final = t + 1 == STEPS
+        if t > 0:
+            h_inside()
+            send_surface(t - 1)
+        if t > 1:
+            far_tick(t - 2)
         arrived(x_now)
         arrived(y_now)
         sent(x_now)
         if t == 0:
-            h_buf[1, 0, PAD : PAD + cy, :] = gx_in[0]
-            h_buf[2, 0, PAD : PAD + cy, :] = gx_in[1]
+            h_buf[1, 0, own, :] = gx_in[0]
+            h_buf[2, 0, own, :] = gx_in[1]
+        h_plane(cx - 1, xh[t, 0], xh[t, 1])
         ex, ey, ez = xt[t, 0], xt[t, 1], xt[t, 2]
-        hy = h_buf[1, 0, PAD : PAD + cy, :]
-        hz = h_buf[2, 0, PAD : PAD + cy, :]
         ahead = rows_up(ex, c1[t, 0:1, :])
-        h_buf[1, 0, PAD : PAD + cy, :] = keep_l * (
-            hy - DTH * ((z_up(ex) - ex) - (e_buf[2, 0, 0:cy, :] - ez))
+        h_buf[1, 0, own, :] = keep_l * (
+            h_buf[1, 0, own, :] - DTH * ((z_up(ex) - ex) - (e_buf[2, 0, 0:cy, :] - ez))
         )
-        h_buf[2, 0, PAD : PAD + cy, :] = keep_l * (
-            hz - DTH * ((e_buf[1, 0, 0:cy, :] - ey) - (ahead - ex))
+        h_buf[2, 0, own, :] = keep_l * (
+            h_buf[2, 0, own, :] - DTH * ((e_buf[1, 0, 0:cy, :] - ey) - (ahead - ex))
         )
         ex, ey, ez = yt[t, 0], yt[t, 1], yt[t, 2]
         ahead = rows_up(ey, c2[t, 0:1, :])
         gy_in[0] = keep_d * (gy_in[0] - DTH * ((syh[t, 1] - ez) - (z_up(ey) - ey)))
         gy_in[1] = keep_d * (gy_in[1] - DTH * ((ahead - ey) - (syh[t, 0] - ex)))
-        e_buf[1, cx, 0:cy, :] = xh[t, 0]
-        e_buf[2, cx, 0:cy, :] = xh[t, 1]
-
-        def edges(x, carry, t=t):
-            e_buf[0, x, cy : cy + 1, :] = yh[t, 0, pl.ds(x, 1), :]
-            e_buf[2, x, cy : cy + 1, :] = yh[t, 1, pl.ds(x, 1), :]
-            h_buf[0, x + 1, PAD - 1 : PAD, :] = gy_in[0, pl.ds(x, 1), :]
-            h_buf[2, x + 1, PAD - 1 : PAD, :] = gy_in[1, pl.ds(x, 1), :]
-            return carry
-
-        lax.fori_loop(0, cx, edges, 0)
-
-        def h_plane(x, carry):
-            own = slice(PAD, PAD + cy)
-            ex, ey, ez = (e_buf[comp, x, 0:cy, :] for comp in range(3))
-            ex_y, ez_y = e_buf[0, x, 1 : cy + 1, :], e_buf[2, x, 1 : cy + 1, :]
-            ey_x, ez_x = e_buf[1, x + 1, 0:cy, :], e_buf[2, x + 1, 0:cy, :]
-            h_buf[0, x + 1, own, :] = h_buf[0, x + 1, own, :] - DTH * ((ez_y - ez) - (z_up(ey) - ey))
-            h_buf[1, x + 1, own, :] = h_buf[1, x + 1, own, :] - DTH * ((z_up(ex) - ex) - (ez_x - ez))
-            h_buf[2, x + 1, own, :] = h_buf[2, x + 1, own, :] - DTH * ((ey_x - ey) - (ex_y - ex))
-            return carry
-
-        lax.fori_loop(0, cx, h_plane, 0)
-
-        def e_plane(x, carry, t=t):
-            own = slice(PAD, PAD + cy)
+        ex, ey, ez = syt[t, 0], syt[t, 1], syt[t, 2]
+        ahead = rows_up(ey, xh[t, 0, cy - 1 : cy, :])
+        hrow[0] = hrow[0] - DTH * ((yh[t, 1] - ez) - (z_up(ey) - ey))
+        hrow[1] = hrow[1] - DTH * ((ahead - ey) - (yh[t, 0] - ex))
+        for x in range(cx):
+            for part, comp in enumerate((0, 2)):
+                h_buf[comp, x + 1, PAD - 1 : PAD, :] = gy_in[part, x : x + 1, :]
+                h_buf[comp, x + 1, PAD + cy - 1 : PAD + cy, :] = hrow[part, x : x + 1, :]
+
+        def e_plane(x, t=t, final=final):
             before = slice(PAD - 1, PAD + cy - 1)
             hx, hy, hz = (h_buf[comp, x + 1, own, :] for comp in range(3))
             hx_y, hz_y = h_buf[0, x + 1, before, :], h_buf[2, x + 1, before, :]
@@ -318,75 +359,61 @@
             mk, fd = mk_buf[cells, :], fd_buf[cells, :]
             ez = ez + mk * (fd - ez)
             fd_buf[cells, :] = fd + (2.0 * mk) * (ez - fd)
+            if final:
+                for comp, value in enumerate((ex, ey, ez, hx, hy, hz)):
+                    fields_out[comp, x] = value
+                return
             e_buf[0, x, 0:cy, :] = ex
             e_buf[1, x, 0:cy, :] = ey
             e_buf[2, x, 0:cy, :] = ez
-            if t + 1 < STEPS:
-                syt[t + 1, 0, pl.ds(x, 1), :] = ex[cy - 1 : cy]
-                syt[t + 1, 1, pl.ds(x, 1), :] = ey[cy - 1 : cy]
-                syt[t + 1, 2, pl.ds(x, 1), :] = ez[cy - 1 : cy]
-                syh[t + 1, 0, pl.ds(x, 1), :] = ex[0:1]
-                syh[t + 1, 1, pl.ds(x, 1), :] = ez[0:1]
-            return carry
-
-        lax.fori_loop(0, cx, e_plane, 0)
-        sent(y_now)
-        if t + 1 < STEPS:
+            syt[t + 1, 0, pl.ds(x, 1), :] = ex[cy - 1 : cy]
+            syt[t + 1, 1, pl.ds(x, 1), :] = ey[cy - 1 : cy]
+            syt[t + 1, 2, pl.ds(x, 1), :] = ez[cy - 1 : cy]
+            syh[t + 1, 0, pl.ds(x, 1), :] = ex[0:1]
+            syh[t + 1, 1, pl.ds(x, 1), :] = ez[0:1]
+
+        if final:
+            e_plane(0)
+            keep_surface(t, fields_out)
+            send_surface(t)
+            planes(1, cx, e_plane)
+            sent(y_now)
+        else:
+            planes(0, cx, e_plane)
             stage_corners(t + 1)
+            sent(y_now)
             y_now = y_copies(t + 1)
             begin(y_now)
             x_now = x_copies(t + 1, e_buf.at[:, cx - 1, 0:cy], e_buf.at[1:3, 0, 0:cy])
             begin(x_now)
-        first = start[0, 0]
-        s_all[t, gy] = row_mask * (
-            e_buf[2, 0, pl.ds(first, SY), :] + h_buf[1, 1, pl.ds(PAD + first, SY), :]
-        )
-        to_peers(lambda peer, t=t: s_all.at[t, gy], s_all.at[t, gy], s_send.at[t], s_recv.at[t])
-
-    stores = [
-        pltpu.make_async_copy(e_buf.at[:, 0:cx, 0:cy], fields_out.at[0:3], out_sem.at[0]),
-        pltpu.make_async_copy(h_buf.at[:, 1 : cx + 1, PAD : PAD + cy], fields_out.at[3:6], out_sem.at[1]),
-    ]
-    for store in stores:
-        store.start()
+            keep_surface(t, e_buf)
 
     for holder in range(n_y):
         for slot in range(slots):
-            cell = target[holder, slot]
+            cell = target[slot, holder]
             line = fd_buf[pl.ds(jnp.maximum(cell, 0), 1), :]
             alive = jnp.broadcast_to(cell, (1, nz)) >= 0
             fback[holder, slot : slot + 1, :] = jnp.where(alive, line, fin[holder, slot : slot + 1, :])
     to_peers(lambda peer: fback.at[peer], fhome.at[gy], f_send.at[1], f_recv.at[1])
     fhome[gy] = fback[gy]
 
-    for t in range(STEPS):
-        wait_all(s_all.at[t], s_recv.at[t])
-        q = jnp.dot(s_all[t].reshape(row_count, nz), table[...], precision=HIGH, preferred_element_type=jnp.float32)
-        q_real, q_imag = q[:, 0:local_a], q[:, local_a : 2 * local_a]
-        g_all[gy, t : t + 1, :] = jnp.sum(q_real * yc[...] - q_imag * ys[...], axis=0, keepdims=True)
-        g_all[gy, STEPS + t : STEPS + t + 1, :] = jnp.sum(q_real * ys[...] + q_imag * yc[...], axis=0, keepdims=True)
+    for t in range(max(0, STEPS - 2), STEPS):
+        far_tick(t)
     to_peers(lambda peer: g_all.at[gy], g_all.at[gy], g_send, g_recv)
     wait_all(fhome, f_recv.at[1])
-    home = pltpu.make_async_copy(fhome, fine_out, out_sem.at[2])
-    home.start()
+    fine_out[...] = fhome[...]
     wait_all(g_all, g_recv)
     weights = w_buf[:, 0 : 2 * STEPS]
     for part in range(n_y):
-        far_buf[:, part * local_a : (part + 1) * local_a] = jnp.dot(
+        far_out[:, part * local_a : (part + 1) * local_a] = jnp.dot(
             weights, g_all[part], precision=HIGH, preferred_element_type=jnp.float32
         )
-    far = pltpu.make_async_copy(far_buf, far_out, out_sem.at[3])
-    far.start()
 
     wait_all(fin, f_send.at[0])
     wait_all(fhome, f_send.at[1])
     for t in range(STEPS + 1):
         wait_all(s_all.at[t], s_send.at[t])
     wait_all(g_all, g_send)
-    for store in stores:
-        store.wait()
-    home.wait()
-    far.wait()
 
 
 def shards(
@@ -400,8 +427,7 @@
     f32 = jnp.float32
     vmem = lambda *shape: pltpu.VMEM(shape, f32)
     dma = pltpu.SemaphoreType.DMA
-    any_space = pl.BlockSpec(memory_space=pl.ANY)
-    smem = pl.BlockSpec(memory_space=pltpu.SMEM)
+    hbm = pl.BlockSpec(memory_space=pltpu.HBM)
     scratch = [
         vmem(3, cx + 1, cy + PAD, nz),
         vmem(3, cx + 1, cy + PAD, nz),
@@ -433,7 +459,14 @@
         vmem(n_y * SY, local_a),
         vmem(2 * freqs, 128),
         vmem(n_y, 2 * STEPS, local_a),
-        vmem(2 * freqs, angles),
+        vmem(2, cx, nz),
+        vmem(1, angles),
+        pltpu.SMEM(ca_table.shape, f32),
+        pltpu.SMEM(cb_table.shape, f32),
+        pltpu.SMEM((slots, n_y), jnp.int32),
+        pltpu.SMEM((1, 1), jnp.int32),
+        pltpu.SMEM((1, 1), jnp.int32),
+        pltpu.SMEM(omega.shape, f32),
         dma((4,)),
         dma((6 * STEPS + 2,)),
         dma((6 * STEPS + 2,)),
@@ -443,7 +476,7 @@
         dma((2,)),
         dma(()),
         dma(()),
-        dma((4,)),
+        dma((7,)),
     ]
     out, fine_new, far = pl.pallas_call(
         functools.partial(kernel, n_x, n_y),
@@ -452,15 +485,15 @@
             jax.ShapeDtypeStruct((n_y, slots, nz), f32),
             jax.ShapeDtypeStruct((2 * freqs, angles), f32),
         ),
-        in_specs=[any_space] * 3 + [pl.BlockSpec(memory_space=pltpu.VMEM)] + [smem] * 6,
-        out_specs=(any_space,) * 3,
+        in_specs=[hbm] * 10,
+        out_specs=(pl.BlockSpec(memory_space=pltpu.VMEM),) * 3,
         scratch_shapes=scratch,
         compiler_params=pltpu.CompilerParams(
             collective_id=0, has_side_effects=True, vmem_limit_bytes=40 * 1024 * 1024
         ),
     )(
         fields, material, fine.reshape(n_y, slots, nz), bearing.reshape(1, angles),
-        ca_table, cb_table, face_target.reshape(n_y, slots), surf_start, surf_count, omega,
+        ca_table, cb_table, face_target.reshape(n_y, slots).T, surf_start, surf_count, omega,
     )
     return out, fine_new.reshape(fine.shape), far.reshape(1, 2, freqs, angles)
 

time: 54.5 us -> 44.5 us (0.82)
  Pallas kernels: 43 us -> 33 us
    pallas_call x1, Pallas kernels: 43 us -> 33 us  [shards(): pl.pallas_call(functools.partial(kernel, n_x, n_y), out_shape=(jax.ShapeD...]
    reshape x1 -> x0, local copies, waits for them, and re-layouts: 0.75 us -> none  [shards(): face_target.reshape(n_y, slots)]
    unnamed x17 -> x19, local copies, waits for them, and re-layouts: 8.45 us -> 9.12 us
where the time goes in v1:
time: 44.5 us; the launch traced here: 44.1 us
  Pallas kernels  33 us (74%)
  local copies, waits for them, and re-layouts  9.12 us (20%)
  between operations  1.95 us (4%)
    pallas_call x1, Pallas kernels, shards(): pl.pallas_call(functools.partial(kernel, n_x, n_y), out_shape=(jax.ShapeD...  33 us
    unnamed x19, local copies, waits for them, and re-layouts  9.12 us

profile of v1, /device:TPU:0, one launch (start us, length us, event | category | flops | bytes accessed | tf_op | source)
XLA Modules:
  0.0 44.1 jit_solution(1308414674803660661)
XLA Ops:
  1.9 0.0 copy-start
  1.9 1.4 %copy-done = f32[6,16,32,128]{3,2,1,0:T(8,128)S(1)} copy-done((f32[6,16,32,128]{3,2,1,0:T(8,128)S(1)}, f32[6,16,32,128]{3,2,1,0:T(8,128)}, u32[]{:S(2)}) %copy-start) | copy-done | bytes 1572888
  3.3 0.0 copy-start.1
  3.3 0.9 %copy-done.1 = s32[16,32,128]{2,1,0:T(8,128)S(1)} copy-done((s32[16,32,128]{2,1,0:T(8,128)S(1)}, s32[16,32,128]{2,1,0:T(8,128)}, u32[]{:S(2)}) %copy-start.1) | copy-done | bytes 262168
  4.3 0.0 copy-start.2
  4.3 0.7 %copy-done.2 = f32[4096]{0:T(1024)S(1)} copy-done((f32[4096]{0:T(1024)S(1)}, f32[4096]{0:T(1024)}, u32[]{:S(2)}) %copy-start.2) | copy-done | bytes 16408
  5.0 0.0 copy-start.3
  5.0 0.7 %copy-done.3 = f32[1,1,8,2,128]{4,3,2,1,0:T(2,128)S(1)} copy-done((f32[1,1,8,2,128]{4,3,2,1,0:T(2,128)S(1)}, f32[1,1,8,2,128]{4,3,2,1,0:T(2,128)}, u32[]{:S(2)}) %copy-start.3) | copy-done | bytes 8216
  5.7 0.0 copy-start.4
  5.7 0.7 %copy-done.4 = s32[1,1,8,2]{2,3,1,0:T(2,128)S(1)} copy-done((s32[1,1,8,2]{2,3,1,0:T(2,128)S(1)}, s32[1,1,8,2]{2,3,1,0:T(2,128)}, u32[]{:S(2)}) %copy-start.4) | copy-done | bytes 88
  6.4 0.0 copy-start.5
  6.4 0.7 %copy-done.5 = f32[16]{0:T(128)S(1)} copy-done((f32[16]{0:T(128)S(1)}, f32[16]{0:T(128)}, u32[]{:S(2)}) %copy-start.5) | copy-done | bytes 88
  7.0 0.0 copy-start.6
  7.0 0.7 %copy-done.6 = f32[16]{0:T(128)S(1)} copy-done((f32[16]{0:T(128)S(1)}, f32[16]{0:T(128)}, u32[]{:S(2)}) %copy-start.6) | copy-done | bytes 88
  7.7 0.0 copy-start.7
  7.7 0.7 %copy-done.7 = f32[32]{0:T(128)S(1)} copy-done((f32[32]{0:T(128)S(1)}, f32[32]{0:T(128)}, u32[]{:S(2)}) %copy-start.7) | copy-done | bytes 152
  8.3 33.0 %shard_map.121 = (f32[6,16,32,128]{3,2,1,0:T(8,128)S(1)}, f32[8,2,128]{2,1,0:T(2,128)S(1)}, f32[64,4096]{1,0:T(8,128)S(1)}) custom-call(f32[6,16,32,128]{3,2,1,0:T(8,128)S(1)} %copy-done, s32[16,32,128]{2,1,0:T(8,128)S(1)} %copy-done.1, f32[8,2,128]{2,1,0:T(2,128)S(1)} %bitcast.9, f32[1,4096]{1,0:T(1,128)S(1)} %bitcast.8, f32[16]{0:T(128)S(1)} %copy-done.5, ...), custom_call_target="tpu_custom_call" | custom-call | tf_op jit(solution)/shard_map/pallas_call | solution.py:481
  41.4 1.1 %copy.18 = f32[6,16,32,128]{3,2,1,0:T(8,128)} copy(f32[6,16,32,128]{3,2,1,0:T(8,128)S(1)} %get-tuple-element.12) | data formatting | bytes 3145728
  42.5 0.6 %copy.19 = f32[1,1,8,2,128]{4,3,2,1,0:T(2,128)} copy(f32[1,1,8,2,128]{4,3,2,1,0:T(2,128)S(1)} %bitcast.10) | data formatting | bytes 16384
  43.1 1.0 %copy.20 = f32[1,2,32,4096]{3,2,1,0:T(8,128)} copy(f32[1,2,32,4096]{3,2,1,0:T(8,128)S(1)} %bitcast.7) | data formatting | bytes 2097152
Async XLA Ops:
  1.9 1.4 %copy-start = (f32[6,16,32,128]{3,2,1,0:T(8,128)S(1)}, f32[6,16,32,128]{3,2,1,0:T(8,128)}, u32[]{:S(2)}) copy-start(f32[6,16,32,128]{3,2,1,0:T(8,128)} %fields.1) | copy-start | bytes 4718596
  3.3 0.9 %copy-start.1 = (s32[16,32,128]{2,1,0:T(8,128)S(1)}, s32[16,32,128]{2,1,0:T(8,128)}, u32[]{:S(2)}) copy-start(s32[16,32,128]{2,1,0:T(8,128)} %material.1) | copy-start | bytes 786436
  4.3 0.7 %copy-start.2 = (f32[4096]{0:T(1024)S(1)}, f32[4096]{0:T(1024)}, u32[]{:S(2)}) copy-start(f32[4096]{0:T(1024)} %param.19) | copy-start | bytes 49156
  5.0 0.7 %copy-start.3 = (f32[1,1,8,2,128]{4,3,2,1,0:T(2,128)S(1)}, f32[1,1,8,2,128]{4,3,2,1,0:T(2,128)}, u32[]{:S(2)}) copy-start(f32[1,1,8,2,128]{4,3,2,1,0:T(2,128)} %param.14) | copy-start | bytes 24580
  5.7 0.7 %copy-start.4 = (s32[1,1,8,2]{2,3,1,0:T(2,128)S(1)}, s32[1,1,8,2]{2,3,1,0:T(2,128)}, u32[]{:S(2)}) copy-start(s32[1,1,8,2]{2,3,1,0:T(2,128)} %param.15) | copy-start | bytes 196
  6.4 0.7 %copy-start.5 = (f32[16]{0:T(128)S(1)}, f32[16]{0:T(128)}, u32[]{:S(2)}) copy-start(f32[16]{0:T(128)} %ca_in.1) | copy-start | bytes 196
  7.0 0.7 %copy-start.6 = (f32[16]{0:T(128)S(1)}, f32[16]{0:T(128)}, u32[]{:S(2)}) copy-start(f32[16]{0:T(128)} %cb_in.1) | copy-start | bytes 196
  7.7 0.7 %copy-start.7 = (f32[32]{0:T(128)S(1)}, f32[32]{0:T(128)}, u32[]{:S(2)}) copy-start(f32[32]{0:T(128)} %omega_in.1) | copy-start | bytes 388

commit v2 on v1

--- a/solution.py
+++ b/solution.py
@@ -206,7 +206,7 @@
         h_buf[1, x + 1, own, :] = h_buf[1, x + 1, own, :] - DTH * ((z_up(ex) - ex) - (ez_x - ez))
         h_buf[2, x + 1, own, :] = h_buf[2, x + 1, own, :] - DTH * ((ey_x - ey) - (ex_y - ex))
 
-    def planes(first, last, one, most=5):
+    def planes(first, last, one, most=16):
         group = max(k for k in range(1, most + 1) if (last - first) % k == 0)
 
         def several(index, carry):
@@ -489,12 +489,26 @@
         out_specs=(pl.BlockSpec(memory_space=pltpu.VMEM),) * 3,
         scratch_shapes=scratch,
         compiler_params=pltpu.CompilerParams(
-            collective_id=0, has_side_effects=True, vmem_limit_bytes=40 * 1024 * 1024
+            collective_id=0, has_side_effects=True, vmem_limit_bytes=60 * 1024 * 1024
         ),
     )(
         fields, material, fine.reshape(n_y, slots, nz), bearing.reshape(1, angles),
         ca_table, cb_table, face_target.reshape(n_y, slots).T, surf_start, surf_count, omega,
     )
+    def hand_on(a, b, c, a_out, b_out, c_out, sems):
+        copies = [pltpu.make_async_copy(p, q, sems.at[k]) for k, (p, q) in enumerate(((a, a_out), (b, b_out), (c, c_out)))]
+        for copy in copies:
+            copy.start()
+        for copy in copies:
+            copy.wait()
+
+    out, fine_new, far = pl.pallas_call(
+        hand_on,
+        out_shape=tuple(jax.ShapeDtypeStruct(v.shape, f32) for v in (out, fine_new, far)),
+        in_specs=[pl.BlockSpec(memory_space=pltpu.VMEM)] * 3,
+        out_specs=(hbm,) * 3,
+        scratch_shapes=[dma((3,))],
+    )(out, fine_new, far)
     return out, fine_new.reshape(fine.shape), far.reshape(1, 2, freqs, angles)
 
 

time: 44.5 us -> 39.3 us (0.88)
  local copies, waits for them, and re-layouts: 9.12 us -> 0 us
  Pallas kernels: 33 us -> 37.2 us
    unnamed x19 -> x0, local copies, waits for them, and re-layouts: 9.12 us -> none
    pallas_call x0 -> x1, Pallas kernels: none -> 3.23 us  [shards(): pl.pallas_call(hand_on, out_shape=tuple((jax.ShapeDtypeStruct(v.shape, f3...]
    pallas_call x1, Pallas kernels: 33 us -> 34 us  [shards(): pl.pallas_call(functools.partial(kernel, n_x, n_y), out_shape=(jax.ShapeD...]
where the time goes in v2:
time: 39.3 us; the launch traced here: 39.2 us
  Pallas kernels  37.2 us (95%)
  between operations  1.93 us (5%)
    pallas_call x1, Pallas kernels, shards(): pl.pallas_call(functools.partial(kernel, n_x, n_y), out_shape=(jax.ShapeD...  34 us
    pallas_call x1, Pallas kernels, shards(): pl.pallas_call(hand_on, out_shape=tuple((jax.ShapeDtypeStruct(v.shape, f3...  3.23 us

profile of v2, /device:TPU:0, one launch (start us, length us, event | category | flops | bytes accessed | tf_op | source)
XLA Modules:
  0.0 39.2 jit_solution(6366488159806165430)
XLA Ops:
  1.9 34.0 %shard_map.121 = (f32[6,16,32,128]{3,2,1,0:T(8,128)}, f32[8,2,128]{2,1,0:T(2,128)}, f32[64,4096]{1,0:T(8,128)}) custom-call(f32[6,16,32,128]{3,2,1,0:T(8,128)} %fields.1, s32[16,32,128]{2,1,0:T(8,128)} %material.1, f32[8,2,128]{2,1,0:T(2,128)} %bitcast.8, f32[1,4096]{1,0:T(1,128)} %bitcast.7, f32[16]{0:T(128)} %ca_in.1, f32[16]{0:T(128)} %cb_in.1, ...), custom_call_target="tpu_custom_call" | custom-call | tf_op jit(solution)/shard_map/pallas_call | solution.py:481
  35.9 3.2 %shard_map.122 = (f32[6,16,32,128]{3,2,1,0:T(8,128)}, f32[8,2,128]{2,1,0:T(2,128)}, f32[64,4096]{1,0:T(8,128)}) custom-call(f32[6,16,32,128]{3,2,1,0:T(8,128)} %get-tuple-element.9.a, f32[8,2,128]{2,1,0:T(2,128)} %get-tuple-element.10.b, f32[64,4096]{1,0:T(8,128)} %get-tuple-element.11.c), custom_call_target="tpu_custom_call" | custom-call | tf_op jit(solution)/shard_map/pallas_call | solution.py:505
